TPU v7x, 512 devices: a whole 4x8x8 slice. The times are simulated.
512 devices in a mesh: gx: 64 (over y_hi, z, core), gy: 8 (over y_lo, x).
Axes of the slice: x: 4, y: 8 (y_hi: 4, y_lo: 2; y = y_hi * 2 + y_lo), z: 8, core: 2. Of those that a mesh axis runs over, the one named last changes fastest.
Arguments:
- gas_state: float32 [5, 512, 64, 1024], P(None, 'gx', 'gy'), may hold values from -6 to 6
- mixing: float32 [512, 64, 1024], P('gx', 'gy'), may hold values from 0.02 to 0.15
- particles: float32 [8, 1048576], P(None, ('gx', 'gy')), as said below
- cell_index: int32 [1048576], P(('gx', 'gy')), may hold values from 0 to 65535
- size_class: int32 [1048576], P(('gx', 'gy')), may hold values from 0 to 6
- destination: int32 [1048576], P(('gx', 'gy')), may hold values from 0 to 8, as said below
- slot: int32 [1048576], P(('gx', 'gy')), may hold values from 0 to 127, as said below
- drag_rate: float32 [7], replicated, may hold values from 0.1 to 2
- settling: float32 [7], replicated, may hold values from 0.3 to 3
- heat_rate: float32 [7], replicated, may hold values from 0.05 to 1
Outputs:
- gas_next: float32 [5, 512, 64, 1024], P(None, 'gx', 'gy')
- kept: float32 [8, 1048576], P(None, ('gx', 'gy'))
- arrived: float32 [8, 8, 65536], P(None, None, ('gx', 'gy'))
Inputs may be any that keep to these rules, and one draw needn't show every extreme that they name: Destinations 1 to 8 follow the order of the steps; each tile sends to every destination between 1 and 128 particles, and in every draw each tile sends exactly 128 to one destination. Moving particles of one tile with one destination take distinct slots 0 to count - 1; staying particles have slot 0. `particles`: attribute 7 (mass) lies in 0.25 to 2.
All inputs are finite; a program needn't handle non-finite values.
Results may differ from a plain program's by a relative error of at most 0.0001.
Values sent between devices are 32-bit elements; how exact they have to be, the bound alone decides.
A program may use at most 64 MiB of HBM per device.

v0:
```python
import functools

import jax
import jax.numpy as jnp
from jax import lax
from jax.experimental import pallas as pl
from jax.experimental.pallas import tpu as pltpu
from jax.sharding import PartitionSpec as P

MESH = pl.DeviceIdType.MESH
STEPS = ((-1, -1), (-1, 0), (-1, 1), (0, -1), (0, 1), (1, -1), (1, 0), (1, 1))
F32, BF16 = jnp.float32, jnp.bfloat16
BLOCK = 256
CHUNK = 256


def split2(x):
    hi = x.astype(BF16)
    return hi, (x - hi.astype(F32)).astype(BF16)


def kernel(
    remote,
    gas, mixing, grains, cell, kind, dest, slot, drag_h, settle_h, heat_h,
    out_v, kept_v, landing,
    gas_v, mix_v, grain_v, cell_v, kind_v, dest_v, slot_v,
    pieces, hot, fluid, weighted, edge_y, halo_x, halo_y, sending, drag_t, settle_t, heat_t,
    load_sem, send_sem, recv_sem,
):
    comps, si, sj, levels = gas.shape
    cols = si * sj
    slots = grains.shape[1]
    capacity = landing.shape[2]
    nx, ny = remote
    if nx > 1:
        ix, iy = lax.axis_index("gx"), lax.axis_index("gy")

        def at(dx, dy):
            return (lax.rem(ix + dx + nx, nx), lax.rem(iy + dy + ny, ny))

        barrier = pltpu.get_barrier_semaphore()
        for dx, dy in STEPS:
            pl.semaphore_signal(barrier, inc=1, device_id=at(dx, dy), device_id_type=MESH)

    loads = [
        pltpu.make_async_copy(src, dst, load_sem.at[n])
        for n, (src, dst) in enumerate(
            ((cell, cell_v), (gas, gas_v), (grains, grain_v), (kind, kind_v), (dest, dest_v), (slot, slot_v), (mixing, mix_v),
             (drag_h, drag_t), (settle_h, settle_t), (heat_h, heat_t))
        )
    ]
    for load in loads:
        load.start()

    loads[0].wait()
    for n in range(slots // BLOCK):
        span = slice(n * BLOCK, (n + 1) * BLOCK)
        level = cell_v[:, span] & (levels - 1)
        rows = lax.broadcasted_iota(jnp.int32, (levels, BLOCK), 0)
        hot[:, span] = jnp.where(rows == level, 1.0, 0.0).astype(BF16)

    copies = []
    if nx > 1:
        pl.semaphore_wait(barrier, len(STEPS))
        for side, (row, step) in enumerate(((si - 1, 1), (0, -1))):
            copies.append(
                pltpu.make_async_remote_copy(
                    gas.at[:, row], halo_x.at[side], send_sem.at[side], recv_sem.at[side], at(step, 0), MESH
                )
            )
            copies[-1].start()
    loads[1].wait()
    for side, (row, step) in enumerate(((sj - 1, 1), (0, -1))):
        for c in range(comps):
            edge_y[side, c] = gas_v[c, :, row, :]
        if nx > 1:
            copies.append(
                pltpu.make_async_remote_copy(
                    edge_y.at[side], halo_y.at[side], send_sem.at[2 + side], recv_sem.at[2 + side], at(0, step), MESH
                )
            )
            copies[-1].start()

    for c in range(4):
        hi, lo = split2(gas_v[c].reshape(cols, levels))
        pieces[c * cols : (c + 1) * cols, :] = hi
        pieces[(4 + c) * cols : (5 + c) * cols, :] = lo
    for n in range(slots // BLOCK):
        span = slice(n * BLOCK, (n + 1) * BLOCK)
        picked = jnp.dot(pieces[...], hot[:, span], preferred_element_type=F32)
        picked = picked[: 4 * cols] + picked[4 * cols :]
        column = cell_v[:, span] // levels
        mask = lax.broadcasted_iota(jnp.int32, (cols, BLOCK), 0) == column
        for c in range(4):
            fluid[c : c + 1, span] = jnp.sum(
                jnp.where(mask, picked[c * cols : (c + 1) * cols], 0.0), axis=0, keepdims=True
            )

    for load in loads[2:]:
        load.wait()
    kinds = kind_v[...]
    drag = jnp.zeros(kinds.shape, F32)
    fall = jnp.zeros(kinds.shape, F32)
    heat = jnp.zeros(kinds.shape, F32)
    for k in range(drag_t.shape[0]):
        drag = jnp.where(kinds == k, drag_t[k], drag)
        fall = jnp.where(kinds == k, settle_t[k], fall)
        heat = jnp.where(kinds == k, heat_t[k], heat)
    now = grain_v[...]
    row = lax.broadcasted_iota(jnp.int32, now.shape, 0)
    rate = jnp.where(row == 6, heat, drag)
    target = jnp.where(row == 6, fluid[3:4, :], fluid[2:3, :] - fall)
    target = jnp.where(row == 3, fluid[0:1, :], jnp.where(row == 4, fluid[1:2, :], target))
    after = (now + rate * target) / (1.0 + rate)
    moved = now + pltpu.roll(after, 5, 0)
    new = jnp.where(row < 3, moved, jnp.where(row == 7, now, after))
    force = now[7:8] * (now - after)
    dests = dest_v[...]
    kept_v[...] = jnp.where(dests == 0, new, 0.0)
    first = jnp.where(dests <= 3, -1.0, jnp.where(dests >= 6, 1.0, 0.0))
    second = jnp.where(
        (dests == 1) | (dests == 4) | (dests == 6), -1.0, jnp.where((dests == 3) | (dests == 5) | (dests == 8), 1.0, 0.0)
    )
    sent = new - jnp.where(row == 0, first * si, jnp.where(row == 1, second * sj, 0.0))

    s0 = sent.astype(BF16).astype(F32)
    s1 = (sent - s0).astype(BF16).astype(F32)
    s2 = sent - s0 - s1
    left = jnp.concatenate(
        [jnp.where(dests == d + 1, s, 0.0) for s in (s0, s1, s2) for d in range(8)], axis=0
    ).astype(BF16)
    slot_hot = jnp.where(
        lax.broadcasted_iota(jnp.int32, (capacity, slots), 0) == slot_v[...], 1.0, 0.0
    ).astype(BF16)
    packed = lax.dot_general(left, slot_hot, (((1,), (1,)), ((), ())), preferred_element_type=F32)
    sending[...] = (packed[:64] + packed[64:128] + packed[128:]).reshape(8, 8, capacity)
    if nx > 1:
        for d, (dx, dy) in enumerate(STEPS):
            copies.append(
                pltpu.make_async_remote_copy(
                    sending.at[d], landing.at[d], send_sem.at[4 + d], recv_sem.at[4 + d], at(dx, dy), MESH
                )
            )
            copies[-1].start()

    f0 = force.astype(BF16).astype(F32)
    f1 = force - f0
    column = cell_v[...] // levels
    mask = lax.broadcasted_iota(jnp.int32, (cols, slots), 0) == column
    for k, f in enumerate((f0, f1)):
        for c in range(4):
            weighted[(4 * k + c) * cols : (4 * k + c + 1) * cols, :] = jnp.where(mask, f[3 + c : 4 + c], 0.0).astype(BF16)

    for copy in copies[:4]:
        copy.wait()
    for side in range(2):
        if nx > 1:
            outside_x = ix == (0 if side == 0 else nx - 1)
            outside_y = iy == (0 if side == 0 else ny - 1)
            halo_x[side] = jnp.where(outside_x, 0.0, halo_x[side])
            halo_y[side] = jnp.where(outside_y, 0.0, halo_y[side])

    wide = CHUNK + 256
    for n in range(levels // CHUNK):
        lo, hi = n * CHUNK, (n + 1) * CHUNK
        dep = lax.dot_general(
            weighted[...], hot[lo:hi, :], (((1,), (1,)), ((), ())), preferred_element_type=F32
        )
        dep = (dep[: 4 * cols] + dep[4 * cols :]).reshape(4, si, sj, CHUNK)
        jrow = lax.broadcasted_iota(jnp.int32, (sj, CHUNK), 0)
        lane = lax.broadcasted_iota(jnp.int32, (sj, CHUNK), 1)
        for c in range(comps):
            for i in range(si):
                here = gas_v[c, i, :, lo:hi]
                before = halo_x[0, c, :, lo:hi] if i == 0 else gas_v[c, i - 1, :, lo:hi]
                behind = halo_x[1, c, :, lo:hi] if i == si - 1 else gas_v[c, i + 1, :, lo:hi]
                left_j = jnp.where(jrow == 0, halo_y[0, c, i : i + 1, lo:hi], pltpu.roll(here, 1, 0))
                right_j = jnp.where(jrow == sj - 1, halo_y[1, c, i : i + 1, lo:hi], pltpu.roll(here, sj - 1, 0))
                below = gas_v[c, i, :, lo - 128 : lo] if lo > 0 else None
                above = gas_v[c, i, :, hi : hi + 128] if hi < levels else None
                zeros = jnp.zeros((sj, 128), F32)
                full = jnp.concatenate([zeros if below is None else below, here, zeros if above is None else above], axis=1)
                down = pltpu.roll(full, 1, 1)[:, 128 : 128 + CHUNK]
                up = pltpu.roll(full, wide - 1, 1)[:, 128 : 128 + CHUNK]
                beside = before + behind + left_j + right_j + down + up
                value = here + mix_v[i, :, lo:hi] * (beside - 6.0 * here)
                if c < 4:
                    value = value + dep[c, i]
                out_v[c, i, :, lo:hi] = value

    for copy in copies[4:]:
        copy.wait()
    if nx > 1:
        for d, (dx, dy) in enumerate(STEPS):
            from_x, from_y = ix - dx, iy - dy
            outside = (from_x < 0) | (from_x >= nx) | (from_y < 0) | (from_y >= ny)
            landing[d] = jnp.where(outside, 0.0, landing[d])
    else:
        landing[...] = sending[...]


def write_out(a, b, c, out_a, out_b, out_c, sems):
    copies = [
        pltpu.make_async_copy(src, dst, sems.at[n]) for n, (src, dst) in enumerate(((a, out_a), (b, out_b), (c, out_c)))
    ]
    for copy in copies:
        copy.start()
    for copy in copies:
        copy.wait()


def on_device(remote, gas, mixing, grains, cell, kind, dest, slot, drag, settle, heat):
    comps, si, sj, levels = gas.shape
    attrs, slots = grains.shape
    capacity = slots // 16
    row = (1, slots)
    hbm = pl.BlockSpec(memory_space=pltpu.HBM)
    vmem = pl.BlockSpec(memory_space=pltpu.VMEM)
    held = tuple(pltpu.with_memory_space_constraint(x, pltpu.HBM) for x in (
        gas, mixing, grains, cell.reshape(row), kind.reshape(row), dest.reshape(row), slot.reshape(row), drag, settle, heat))
    results = pl.pallas_call(
        functools.partial(kernel, remote),
        out_shape=(
            pltpu.VMEM(gas.shape, F32),
            pltpu.VMEM(grains.shape, F32),
            pltpu.VMEM((8, attrs, capacity), F32),
        ),
        in_specs=[hbm] * 10,
        out_specs=(vmem,) * 3,
        scratch_shapes=[
            pltpu.VMEM(gas.shape, F32),
            pltpu.VMEM(mixing.shape, F32),
            pltpu.VMEM(grains.shape, F32),
            pltpu.VMEM(row, jnp.int32),
            pltpu.VMEM(row, jnp.int32),
            pltpu.VMEM(row, jnp.int32),
            pltpu.VMEM(row, jnp.int32),
            pltpu.VMEM((8 * si * sj, levels), BF16),
            pltpu.VMEM((levels, slots), BF16),
            pltpu.VMEM((8, slots), F32),
            pltpu.VMEM((8 * si * sj, slots), BF16),
            pltpu.VMEM((2, comps, si, levels), F32),
            pltpu.VMEM((2, comps, sj, levels), F32),
            pltpu.VMEM((2, comps, si, levels), F32),
            pltpu.VMEM((8, attrs, capacity), F32),
            pltpu.SMEM(drag.shape, F32),
            pltpu.SMEM(settle.shape, F32),
            pltpu.SMEM(heat.shape, F32),
            pltpu.SemaphoreType.DMA((10,)),
            pltpu.SemaphoreType.DMA((12,)),
            pltpu.SemaphoreType.DMA((12,)),
        ],
        compiler_params=pltpu.CompilerParams(
            collective_id=0 if remote[0] > 1 else None,
            has_side_effects=True,
            vmem_limit_bytes=40 * 1024 * 1024,
        ),
        name="ash_step",
    )(*held)
    shapes = tuple(jax.ShapeDtypeStruct(r.shape, F32) for r in results)
    results = tuple(pltpu.with_memory_space_constraint(r, pltpu.VMEM) for r in results)
    return pl.pallas_call(
        write_out,
        out_shape=shapes,
        in_specs=[vmem] * 3,
        out_specs=(hbm,) * 3,
        scratch_shapes=[pltpu.SemaphoreType.DMA((3,))],
        name="write_out",
    )(*results)


def solution(mesh):
    tiles = P(None, ("gx", "gy"))
    per_slot = P(("gx", "gy"))
    return jax.shard_map(
        functools.partial(on_device, (mesh.shape["gx"], mesh.shape["gy"])),
        mesh=mesh,
        in_specs=(P(None, "gx", "gy", None), P("gx", "gy", None), tiles) + (per_slot,) * 4 + (P(),) * 3,
        out_specs=(P(None, "gx", "gy", None), tiles, P(None, None, ("gx", "gy"))),
        check_vma=False,
    )
```

profile of v0, /device:TPU:8, one launch (start us, length us, event | category | flops | bytes accessed | tf_op | source)
XLA Modules:
  0.0 27.8 jit_solution(1741891510423986886)
XLA Ops:
  0.6 26.0 %ash_step.1 = (f32[5,8,8,1024]{3,2,1,0:T(8,128)S(1)}, f32[8,2048]{1,0:T(8,128)S(1)}, f32[8,8,128]{2,1,0:T(8,128)S(1)}) custom-call(f32[5,8,8,1024]{3,2,1,0:T(8,128)} %gas.1, f32[8,8,1024]{2,1,0:T(8,128)} %mixing.1, f32[8,2048]{1,0:T(8,128)} %grains.1, s32[1,2048]{1,0:T(1,128)} %bitcast.4, s32[1,2048]{1,0:T(1,128)} %bitcast.5, s32[1,2048]{1,0:T(1,128)} %bitcast.6, ...), custom_call_target="tpu_custom_call" | custom-call | tf_op jit(solution)/shard_map/ash_step/pallas_call | solution.py:221
  26.7 1.1 %write_out.1 = (f32[5,8,8,1024]{3,2,1,0:T(8,128)}, f32[8,2048]{1,0:T(8,128)}, f32[8,8,128]{2,1,0:T(8,128)}) custom-call(f32[5,8,8,1024]{3,2,1,0:T(8,128)S(1)} %get-tuple-element.6.a, f32[8,2048]{1,0:T(8,128)S(1)} %get-tuple-element.7.b, f32[8,8,128]{2,1,0:T(8,128)S(1)} %get-tuple-element.8.c), custom_call_target="tpu_custom_call" | custom-call | tf_op jit(solution)/shard_map/write_out/pallas_call | solution.py:262
where the time goes:
time: 27.9 us; the launch traced here: 27.8 us
  Pallas kernels  27.1 us (97%)
  between operations  0.64 us (2%)
    pallas_call x1, Pallas kernels, on_device(): pl.pallas_call(functools.partial(kernel, remote), out_shape=(pltpu.VMEM(g...  26 us
    pallas_call x1, Pallas kernels, on_device(): pl.pallas_call(write_out, out_shape=shapes, in_specs=[vmem] * 3, out_spec...  1.1 us

commit v1 on v0

v1 whole, which is shorter than its diff:
```python
import functools

import jax
import jax.numpy as jnp
from jax import lax
from jax.experimental import pallas as pl
from jax.experimental.pallas import tpu as pltpu
from jax.sharding import PartitionSpec as P

MESH = pl.DeviceIdType.MESH
STEPS = ((-1, -1), (-1, 0), (-1, 1), (0, -1), (0, 1), (1, -1), (1, 0), (1, 1))
F32, BF16, I32 = jnp.float32, jnp.bfloat16, jnp.int32
BLOCK = 256
CHUNK = 256
RUN = 16
NT = (((1,), (1,)), ((), ()))


def split2(x):
    hi = x.astype(BF16)
    return hi, (x - hi.astype(F32)).astype(BF16)


def split3(x):
    first = x.astype(BF16).astype(F32)
    second = (x - first).astype(BF16).astype(F32)
    return first, second, x - first - second


def one_hot(rows, ids):
    return jnp.where(lax.broadcasted_iota(I32, (rows, ids.shape[1]), 0) == ids, 1.0, 0.0).astype(BF16)


def sampled(pieces, hot, column, cols):
    picked = jnp.dot(pieces[...], hot, preferred_element_type=F32)
    picked = picked[: 4 * cols] + picked[4 * cols :]
    mask = lax.broadcasted_iota(I32, (cols, column.shape[1]), 0) == column
    return [
        jnp.sum(jnp.where(mask, picked[c * cols : (c + 1) * cols], 0.0), axis=0, keepdims=True) for c in range(4)
    ]


def updated(now, kinds, fluid, drag_t, settle_t, heat_t):
    drag = jnp.zeros(kinds.shape, F32)
    fall = jnp.zeros(kinds.shape, F32)
    heat = jnp.zeros(kinds.shape, F32)
    for k in range(drag_t.shape[0]):
        drag = jnp.where(kinds == k, drag_t[k], drag)
        fall = jnp.where(kinds == k, settle_t[k], fall)
        heat = jnp.where(kinds == k, heat_t[k], heat)
    row = lax.broadcasted_iota(I32, now.shape, 0)
    rate = jnp.where(row == 6, heat, drag)
    target = jnp.where(row == 6, fluid[3], fluid[2] - fall)
    target = jnp.where(row == 3, fluid[0], jnp.where(row == 4, fluid[1], target))
    after = (now + rate * target) / (1.0 + rate)
    moved = now + pltpu.roll(after, 5, 0)
    new = jnp.where(row < 3, moved, jnp.where(row == 7, now, after))
    return after, new, row


def kernel(
    tiles,
    gas, mixing, grains, cell, kind, dest, slot, drag_h, settle_h, heat_h,
    out_v, kept_v, landing,
    gas_v, mix_v, grain_v, cell_v, kind_v, dest_v, slot_v, drag_t, settle_t, heat_t,
    pieces, hot, fluid, weighted, edge_y, halo_x, halo_y, sending,
    load_sem, send_sem, recv_sem,
):
    comps, si, sj, levels = gas.shape
    cols = si * sj
    slots = grains.shape[1]
    capacity = landing.shape[2]
    nx, ny = tiles
    remote = nx > 1

    if remote:
        ix, iy = lax.axis_index("gx"), lax.axis_index("gy")
        place = lax.rem(ix, RUN)
        early = (place == 0) & (ix > 0)
        late = jnp.logical_not(early)
        last = (place == RUN - 1) & (ix < nx - 1)
        slow = place >= RUN - 2

        def at(step):
            return (lax.rem(ix + step[0] + nx, nx), lax.rem(iy + step[1] + ny, ny))

        def inside(step):
            x, y = ix + step[0], iy + step[1]
            return (x >= 0) & (x < nx) & (y >= 0) & (y < ny)

        def number(flag):
            return flag.astype(I32)

        barrier = pltpu.get_barrier_semaphore()

        def greet(steps, when):
            for step in steps:
                @pl.when(when(step) & inside(step))
                def _():
                    pl.semaphore_signal(barrier, inc=1, device_id=at(step), device_id_type=MESH)

        high = 1 + number(iy > 0) + number(iy < ny - 1)
        greet(STEPS, lambda step: (place + step[0] >= 0) & (place + step[0] < RUN))

    def copy_of(n, src, dst, step):
        return pltpu.make_async_remote_copy(src, dst, send_sem.at[n], recv_sem.at[n], at(step), MESH)

    def halo_copy(n):
        if n < 2:
            side, row = n, (si - 1, 0)[n]
            return copy_of(n, gas.at[:, row], halo_x.at[side], ((1, 0), (-1, 0))[side])
        return copy_of(n, edge_y.at[n - 2], halo_y.at[n - 2], ((0, 1), (0, -1))[n - 2])

    halo_steps = ((1, 0), (-1, 0), (0, 1), (0, -1))

    def grain_copy(d):
        return copy_of(4 + d, sending.at[d], landing.at[d], STEPS[d])

    def send(copy, step, when):
        @pl.when(when & inside(step))
        def _():
            copy.start()

    loads = [
        pltpu.make_async_copy(src, dst, load_sem.at[n])
        for n, (src, dst) in enumerate(
            (
                (grains, grain_v), (cell, cell_v), (kind, kind_v), (dest, dest_v), (slot, slot_v),
                (drag_h, drag_t), (settle_h, settle_t), (heat_h, heat_t),
                (gas.at[0:4], gas_v.at[0:4]), (gas.at[4:5], gas_v.at[4:5]), (mixing, mix_v),
            )
        )
    ]
    for load in loads:
        load.start()

    if remote:
        wide = 1 + number(place > 0) + number(place < RUN - 1) + number(last)
        pl.semaphore_wait(barrier, wide * high - 1)
        send(halo_copy(0), halo_steps[0], True)
        greet(STEPS[:3], lambda step: early)
        greet(STEPS[5:], lambda step: last)
        send(halo_copy(1), halo_steps[1], late)

    for load in loads[:8]:
        load.wait()
    now, kinds, dests, cells = grain_v[...], kind_v[...], dest_v[...], cell_v[...]
    level, column = cells & (levels - 1), cells // levels
    slot_hot = one_hot(capacity, slot_v[...])
    ids = jnp.concatenate(
        [(level & -4), (level & 3), column, kinds + 1, jnp.zeros((4, slots), I32)], axis=0
    ).astype(F32)
    values = split3(now) + (ids,)
    left = jnp.concatenate(
        [jnp.where(dests == d, v, 0.0) for d in (6, 7, 8) for v in values], axis=0
    ).astype(BF16)
    ahead = lax.dot_general(left, slot_hot, NT, preferred_element_type=F32)
    ahead = jnp.concatenate([ahead[32 * d : 32 * (d + 1)] for d in range(3)], axis=1)
    ahead_now = ahead[0:8] + ahead[8:16] + ahead[16:24]
    ahead_ids = ahead[24:32].astype(I32)
    ahead_level = ahead_ids[0:1] + ahead_ids[1:2]
    ahead_hot = one_hot(levels, ahead_level)
    loads[8].wait()
    for c in range(4):
        hi, lo = split2(gas_v[c].reshape(cols, levels))
        pieces[c * cols : (c + 1) * cols, :] = hi
        pieces[(4 + c) * cols : (5 + c) * cols, :] = lo
    ahead_fluid = sampled(pieces, ahead_hot, ahead_ids[2:3], cols)
    _, ahead_new, ahead_row = updated(ahead_now, ahead_ids[3:4] - 1, ahead_fluid, drag_t, settle_t, heat_t)
    ahead_new = jnp.where(ahead_ids[3:4] > 0, ahead_new, 0.0)
    for d in range(5, 8):
        dx, dy = STEPS[d]
        span = slice((d - 5) * capacity, (d - 4) * capacity)
        filled, row = ahead_ids[3:4, span] > 0, ahead_row[:, span]
        shift = jnp.where(row == 0, float(dx * si), jnp.where(row == 1, float(dy * sj), 0.0))
        sending[d] = jnp.where(filled, ahead_new[:, span] - shift, 0.0)
        if remote:
            send(grain_copy(d), STEPS[d], True)

    loads[9].wait()
    for side, row in enumerate((sj - 1, 0)):
        for c in range(comps):
            edge_y[side, c] = gas_v[c, :, row, :]
        if remote:
            send(halo_copy(2 + side), halo_steps[2 + side], jnp.logical_not(slow))

    for n in range(slots // BLOCK):
        span = slice(n * BLOCK, (n + 1) * BLOCK)
        block_hot = one_hot(levels, cell_v[:, span] & (levels - 1))
        hot[:, span] = block_hot
        block_fluid = sampled(pieces, block_hot, cell_v[:, span] // levels, cols)
        for c in range(4):
            fluid[c : c + 1, span] = block_fluid[c]

    after, new, row = updated(now, kinds, [fluid[c : c + 1, :] for c in range(4)], drag_t, settle_t, heat_t)
    force = now[7:8] * (now - after)
    kept_v[...] = jnp.where(dests == 0, new, 0.0)
    first = jnp.where(dests <= 3, -1.0, 0.0)
    second = jnp.where((dests == 1) | (dests == 4), -1.0, jnp.where((dests == 3) | (dests == 5), 1.0, 0.0))
    sent = new - jnp.where(row == 0, first * si, jnp.where(row == 1, second * sj, 0.0))

    left = jnp.concatenate(
        [jnp.where(dests == d, s, 0.0) for s in split3(sent) for d in range(1, 6)] + [jnp.zeros((8, slots), F32)], axis=0
    ).astype(BF16)
    packed = lax.dot_general(left, slot_hot, NT, preferred_element_type=F32)
    packed = packed[:40] + packed[40:80] + packed[80:120]
    for d in range(5):
        sending[d] = packed[8 * d : 8 * (d + 1)]
        if remote:
            send(grain_copy(d), STEPS[d], late if d < 3 else True)
    if remote:
        for n in (2, 3):
            send(halo_copy(n), halo_steps[n], slow)

    f0 = force.astype(BF16).astype(F32)
    mask = lax.broadcasted_iota(I32, (cols, slots), 0) == column
    for k, f in enumerate((f0, force - f0)):
        for c in range(4):
            weighted[(4 * k + c) * cols : (4 * k + c + 1) * cols, :] = jnp.where(mask, f[3 + c : 4 + c], 0.0).astype(BF16)

    loads[10].wait()
    wide = CHUNK + 256
    for n in range(levels // CHUNK):
        lo, hi = n * CHUNK, (n + 1) * CHUNK
        dep = lax.dot_general(weighted[...], hot[lo:hi, :], NT, preferred_element_type=F32)
        dep = (dep[: 4 * cols] + dep[4 * cols :]).reshape(4, si, sj, CHUNK)
        jrow = lax.broadcasted_iota(I32, (sj, CHUNK), 0)
        zeros = jnp.zeros((sj, 128), F32)
        for c in range(comps):
            for i in range(si):
                here = gas_v[c, i, :, lo:hi]
                beside = jnp.where(jrow == 0, 0.0, pltpu.roll(here, 1, 0))
                beside = beside + jnp.where(jrow == sj - 1, 0.0, pltpu.roll(here, sj - 1, 0))
                if i > 0:
                    beside = beside + gas_v[c, i - 1, :, lo:hi]
                if i < si - 1:
                    beside = beside + gas_v[c, i + 1, :, lo:hi]
                below = gas_v[c, i, :, lo - 128 : lo] if lo > 0 else zeros
                above = gas_v[c, i, :, hi : hi + 128] if hi < levels else zeros
                full = jnp.concatenate([below, here, above], axis=1)
                beside = beside + pltpu.roll(full, 1, 1)[:, 128 : 128 + CHUNK]
                beside = beside + pltpu.roll(full, wide - 1, 1)[:, 128 : 128 + CHUNK]
                value = here + mix_v[i, :, lo:hi] * (beside - 6.0 * here)
                if c < 4:
                    value = value + dep[c, i]
                out_v[c, i, :, lo:hi] = value

    if not remote:
        landing[...] = sending[...]
        return

    @pl.when(early)
    def _():
        pl.semaphore_wait(barrier, high)
    send(halo_copy(1), halo_steps[1], early)
    for d in range(3):
        send(grain_copy(d), STEPS[d], early)

    def back(step):
        return (-step[0], -step[1])

    for n in (2, 3):
        @pl.when(inside(back(halo_steps[n])))
        def _():
            halo_copy(n).wait_recv()
            j = (0, sj - 1)[n - 2]
            for c in range(comps):
                for i in range(si):
                    out_v[c, i, j : j + 1, :] = (
                        out_v[c, i, j : j + 1, :] + mix_v[i, j : j + 1, :] * halo_y[n - 2, c, i : i + 1, :]
                    )
    for n in (1, 0):
        @pl.when(inside(back(halo_steps[n])))
        def _():
            halo_copy(n).wait_recv()
            i = (0, si - 1)[n]
            for c in range(comps):
                out_v[c, i] = out_v[c, i] + mix_v[i] * halo_x[n, c]
    for d in range(8):
        came = inside(back(STEPS[d]))

        @pl.when(came)
        def _():
            grain_copy(d).wait_recv()

        @pl.when(jnp.logical_not(came))
        def _():
            landing[d] = jnp.zeros(landing.shape[1:], F32)
    for n in range(4):
        @pl.when(inside(halo_steps[n]))
        def _():
            halo_copy(n).wait_send()
    for d in range(8):
        @pl.when(inside(STEPS[d]))
        def _():
            grain_copy(d).wait_send()


def write_out(a, b, c, out_a, out_b, out_c, sems):
    copies = [
        pltpu.make_async_copy(src, dst, sems.at[n]) for n, (src, dst) in enumerate(((a, out_a), (b, out_b), (c, out_c)))
    ]
    for copy in copies:
        copy.start()
    for copy in copies:
        copy.wait()


def on_device(tiles, gas, mixing, grains, cell, kind, dest, slot, drag, settle, heat):
    comps, si, sj, levels = gas.shape
    attrs, slots = grains.shape
    capacity = slots // 16
    row = (1, slots)
    hbm = pl.BlockSpec(memory_space=pltpu.HBM)
    vmem = pl.BlockSpec(memory_space=pltpu.VMEM)
    held = (gas, mixing, grains, cell.reshape(row), kind.reshape(row), dest.reshape(row), slot.reshape(row), drag, settle, heat)
    held = tuple(pltpu.with_memory_space_constraint(x, pltpu.HBM) for x in held)
    results = pl.pallas_call(
        functools.partial(kernel, tiles),
        out_shape=(
            pltpu.VMEM(gas.shape, F32),
            pltpu.VMEM(grains.shape, F32),
            pltpu.VMEM((8, attrs, capacity), F32),
        ),
        in_specs=[hbm] * 10,
        out_specs=(vmem,) * 3,
        scratch_shapes=[
            pltpu.VMEM(gas.shape, F32),
            pltpu.VMEM(mixing.shape, F32),
            pltpu.VMEM(grains.shape, F32),
            pltpu.VMEM(row, I32),
            pltpu.VMEM(row, I32),
            pltpu.VMEM(row, I32),
            pltpu.VMEM(row, I32),
            pltpu.SMEM(drag.shape, F32),
            pltpu.SMEM(settle.shape, F32),
            pltpu.SMEM(heat.shape, F32),
            pltpu.VMEM((8 * si * sj, levels), BF16),
            pltpu.VMEM((levels, slots), BF16),
            pltpu.VMEM((8, slots), F32),
            pltpu.VMEM((8 * si * sj, slots), BF16),
            pltpu.VMEM((2, comps, si, levels), F32),
            pltpu.VMEM((2, comps, sj, levels), F32),
            pltpu.VMEM((2, comps, si, levels), F32),
            pltpu.VMEM((8, attrs, capacity), F32),
            pltpu.SemaphoreType.DMA((11,)),
            pltpu.SemaphoreType.DMA((12,)),
            pltpu.SemaphoreType.DMA((12,)),
        ],
        compiler_params=pltpu.CompilerParams(
            collective_id=0 if tiles[0] > 1 else None,
            has_side_effects=True,
            vmem_limit_bytes=40 * 1024 * 1024,
        ),
        name="ash_step",
    )(*held)
    shapes = tuple(jax.ShapeDtypeStruct(r.shape, F32) for r in results)
    results = tuple(pltpu.with_memory_space_constraint(r, pltpu.VMEM) for r in results)
    return pl.pallas_call(
        write_out,
        out_shape=shapes,
        in_specs=[vmem] * 3,
        out_specs=(hbm,) * 3,
        scratch_shapes=[pltpu.SemaphoreType.DMA((3,))],
        name="write_out",
    )(*results)


def solution(mesh):
    tiles = P(None, ("gx", "gy"))
    per_slot = P(("gx", "gy"))
    return jax.shard_map(
        functools.partial(on_device, (mesh.shape["gx"], mesh.shape["gy"])),
        mesh=mesh,
        in_specs=(P(None, "gx", "gy", None), P("gx", "gy", None), tiles) + (per_slot,) * 4 + (P(),) * 3,
        out_specs=(P(None, "gx", "gy", None), tiles, P(None, None, ("gx", "gy"))),
        check_vma=False,
    )
```

time: 27.9 us -> 22.5 us (0.81)
  the two profiles are of different devices: /device:TPU:8 before, /device:TPU:56 now
where the time goes in v1:
time: 22.5 us; the launch traced here: 22.3 us
  Pallas kernels  21.7 us (96%)
  between operations  0.64 us (3%)
    pallas_call x1, Pallas kernels, on_device(): pl.pallas_call(functools.partial(kernel, tiles), out_shape=(pltpu.VMEM(ga...  20.6 us
    pallas_call x1, Pallas kernels, on_device(): pl.pallas_call(write_out, out_shape=shapes, in_specs=[vmem] * 3, out_spec...  1.1 us

profile of v1, /device:TPU:56, one launch (start us, length us, event | category | flops | bytes accessed | tf_op | source)
XLA Modules:
  0.0 22.3 jit_solution(6436838341914220947)
XLA Ops:
  0.6 20.6 %ash_step.1 = (f32[5,8,8,1024]{3,2,1,0:T(8,128)S(1)}, f32[8,2048]{1,0:T(8,128)S(1)}, f32[8,8,128]{2,1,0:T(8,128)S(1)}) custom-call(f32[5,8,8,1024]{3,2,1,0:T(8,128)} %gas.1, f32[8,8,1024]{2,1,0:T(8,128)} %mixing.1, f32[8,2048]{1,0:T(8,128)} %grains.1, s32[1,2048]{1,0:T(1,128)} %bitcast.4, s32[1,2048]{1,0:T(1,128)} %bitcast.5, s32[1,2048]{1,0:T(1,128)} %bitcast.6, ...), custom_call_target="tpu_custom_call" | custom-call | tf_op jit(solution)/shard_map/ash_step/pallas_call | solution.py:318
  21.2 1.1 %write_out.1 = (f32[5,8,8,1024]{3,2,1,0:T(8,128)}, f32[8,2048]{1,0:T(8,128)}, f32[8,8,128]{2,1,0:T(8,128)}) custom-call(f32[5,8,8,1024]{3,2,1,0:T(8,128)S(1)} %get-tuple-element.6.a, f32[8,2048]{1,0:T(8,128)S(1)} %get-tuple-element.7.b, f32[8,8,128]{2,1,0:T(8,128)S(1)} %get-tuple-element.8.c), custom_call_target="tpu_custom_call" | custom-call | tf_op jit(solution)/shard_map/write_out/pallas_call | solution.py:359

commit v2 on v1

--- a/solution.py
+++ b/solution.py
@@ -64,7 +64,7 @@
     out_v, kept_v, landing,
     gas_v, mix_v, grain_v, cell_v, kind_v, dest_v, slot_v, drag_t, settle_t, heat_t,
     pieces, hot, fluid, weighted, edge_y, halo_x, halo_y, sending,
-    load_sem, send_sem, recv_sem,
+    load_sem, send_sem, recv_sem, reply_sem, answer_sem,
 ):
     comps, si, sj, levels = gas.shape
     cols = si * sj
@@ -76,9 +76,11 @@
     if remote:
         ix, iy = lax.axis_index("gx"), lax.axis_index("gy")
         place = lax.rem(ix, RUN)
+        follows = ix < (nx // RUN - 1) * RUN
         early = (place == 0) & (ix > 0)
         late = jnp.logical_not(early)
-        last = (place == RUN - 1) & (ix < nx - 1)
+        last = (place == RUN - 1) & follows
+        usual = jnp.logical_not(last)
         slow = place >= RUN - 2
 
         def at(step):
@@ -93,14 +95,18 @@
 
         barrier = pltpu.get_barrier_semaphore()
 
-        def greet(steps, when):
-            for step in steps:
+        def greet(steps, when, semaphore):
+            for n, step in enumerate(steps):
                 @pl.when(when(step) & inside(step))
                 def _():
-                    pl.semaphore_signal(barrier, inc=1, device_id=at(step), device_id_type=MESH)
+                    pl.semaphore_signal(semaphore(n), inc=1, device_id=at(step), device_id_type=MESH)
+
+        def first_round(step):
+            target = place + step[0]
+            return usual & (target >= 0) & (target < jnp.where(follows, RUN - 1, RUN)) | (early & (step[0] < 0))
 
         high = 1 + number(iy > 0) + number(iy < ny - 1)
-        greet(STEPS, lambda step: (place + step[0] >= 0) & (place + step[0] < RUN))
+        greet(STEPS, first_round, lambda n: barrier)
 
     def copy_of(n, src, dst, step):
         return pltpu.make_async_remote_copy(src, dst, send_sem.at[n], recv_sem.at[n], at(step), MESH)
@@ -135,12 +141,13 @@
         load.start()
 
     if remote:
-        wide = 1 + number(place > 0) + number(place < RUN - 1) + number(last)
-        pl.semaphore_wait(barrier, wide * high - 1)
+        wide = 1 + number(place > 0) + number(place < RUN - 1)
+        pl.semaphore_wait(barrier, jnp.where(last, high, wide * high - 1))
         send(halo_copy(0), halo_steps[0], True)
-        greet(STEPS[:3], lambda step: early)
-        greet(STEPS[5:], lambda step: last)
-        send(halo_copy(1), halo_steps[1], late)
+        greet(STEPS[5:], lambda step: last, lambda n: reply_sem.at[n])
+        greet(STEPS[:3], lambda step: last, lambda n: barrier)
+        greet(STEPS[5:], lambda step: (place == RUN - 2) & follows, lambda n: answer_sem)
+        send(halo_copy(1), halo_steps[1], late & usual)
 
     for load in loads[:8]:
         load.wait()
@@ -177,6 +184,11 @@
         if remote:
             send(grain_copy(d), STEPS[d], True)
 
+    if remote:
+        @pl.when(last)
+        def _():
+            pl.semaphore_wait(answer_sem, high)
+        send(halo_copy(1), halo_steps[1], last)
     loads[9].wait()
     for side, row in enumerate((sj - 1, 0)):
         for c in range(comps):
@@ -249,11 +261,13 @@
         landing[...] = sending[...]
         return
 
-    @pl.when(early)
-    def _():
-        pl.semaphore_wait(barrier, high)
-    send(halo_copy(1), halo_steps[1], early)
-    for d in range(3):
+    for n in (1, 0, 2):
+        @pl.when(early & inside((-1, -STEPS[5 + n][1])))
+        def _():
+            pl.semaphore_wait(reply_sem.at[n], 1)
+        d = 2 - n
+        if n == 1:
+            send(halo_copy(1), halo_steps[1], early)
         send(grain_copy(d), STEPS[d], early)
 
     def back(step):
@@ -346,6 +360,8 @@
             pltpu.SemaphoreType.DMA((11,)),
             pltpu.SemaphoreType.DMA((12,)),
             pltpu.SemaphoreType.DMA((12,)),
+            pltpu.SemaphoreType.REGULAR((3,)),
+            pltpu.SemaphoreType.REGULAR,
         ],
         compiler_params=pltpu.CompilerParams(
             collective_id=0 if tiles[0] > 1 else None,

time: 22.5 us -> 21.5 us (0.956)
  Pallas kernels: 21.7 us -> 20.7 us
    pallas_call x1, Pallas kernels: 20.6 us -> 19.6 us  [on_device(): pl.pallas_call(functools.partial(kernel, tiles), out_shape=(pltpu.VMEM(ga...]
where the time goes in v2:
time: 21.5 us; the launch traced here: 21.3 us
  Pallas kernels  20.7 us (96%)
  between operations  0.64 us (3%)
    pallas_call x1, Pallas kernels, on_device(): pl.pallas_call(functools.partial(kernel, tiles), out_shape=(pltpu.VMEM(ga...  19.6 us
    pallas_call x1, Pallas kernels, on_device(): pl.pallas_call(write_out, out_shape=shapes, in_specs=[vmem] * 3, out_spec...  1.1 us

profile of v2, /device:TPU:56, one launch (start us, length us, event | category | flops | bytes accessed | tf_op | source)
XLA Modules:
  0.0 21.3 jit_solution(14565327581849683034)
XLA Ops:
  0.6 19.6 %ash_step.1 = (f32[5,8,8,1024]{3,2,1,0:T(8,128)S(1)}, f32[8,2048]{1,0:T(8,128)S(1)}, f32[8,8,128]{2,1,0:T(8,128)S(1)}) custom-call(f32[5,8,8,1024]{3,2,1,0:T(8,128)} %gas.1, f32[8,8,1024]{2,1,0:T(8,128)} %mixing.1, f32[8,2048]{1,0:T(8,128)} %grains.1, s32[1,2048]{1,0:T(1,128)} %bitcast.4, s32[1,2048]{1,0:T(1,128)} %bitcast.5, s32[1,2048]{1,0:T(1,128)} %bitcast.6, ...), custom_call_target="tpu_custom_call" | custom-call | tf_op jit(solution)/shard_map/ash_step/pallas_call | solution.py:332
  20.2 1.1 %write_out.1 = (f32[5,8,8,1024]{3,2,1,0:T(8,128)}, f32[8,2048]{1,0:T(8,128)}, f32[8,8,128]{2,1,0:T(8,128)}) custom-call(f32[5,8,8,1024]{3,2,1,0:T(8,128)S(1)} %get-tuple-element.6.a, f32[8,2048]{1,0:T(8,128)S(1)} %get-tuple-element.7.b, f32[8,8,128]{2,1,0:T(8,128)S(1)} %get-tuple-element.8.c), custom_call_target="tpu_custom_call" | custom-call | tf_op jit(solution)/shard_map/write_out/pallas_call | solution.py:375

commit v3 on v2

--- a/solution.py
+++ b/solution.py
@@ -13,6 +13,7 @@
 BLOCK = 256
 CHUNK = 256
 RUN = 16
+FIRST = 3
 NT = (((1,), (1,)), ((), ()))
 
 
@@ -112,12 +113,15 @@
         return pltpu.make_async_remote_copy(src, dst, send_sem.at[n], recv_sem.at[n], at(step), MESH)
 
     def halo_copy(n):
-        if n < 2:
-            side, row = n, (si - 1, 0)[n]
-            return copy_of(n, gas.at[:, row], halo_x.at[side], ((1, 0), (-1, 0))[side])
+        if n == 0:
+            return copy_of(0, gas.at[:FIRST, si - 1], halo_x.at[0, :FIRST], (1, 0))
+        if n == 4:
+            return copy_of(12, gas.at[FIRST:, si - 1], halo_x.at[0, FIRST:], (1, 0))
+        if n == 1:
+            return copy_of(1, gas.at[:, 0], halo_x.at[1], (-1, 0))
         return copy_of(n, edge_y.at[n - 2], halo_y.at[n - 2], ((0, 1), (0, -1))[n - 2])
 
-    halo_steps = ((1, 0), (-1, 0), (0, 1), (0, -1))
+    halo_steps = ((1, 0), (-1, 0), (0, 1), (0, -1), (1, 0))
 
     def grain_copy(d):
         return copy_of(4 + d, sending.at[d], landing.at[d], STEPS[d])
@@ -162,27 +166,29 @@
         [jnp.where(dests == d, v, 0.0) for d in (6, 7, 8) for v in values], axis=0
     ).astype(BF16)
     ahead = lax.dot_general(left, slot_hot, NT, preferred_element_type=F32)
-    ahead = jnp.concatenate([ahead[32 * d : 32 * (d + 1)] for d in range(3)], axis=1)
-    ahead_now = ahead[0:8] + ahead[8:16] + ahead[16:24]
-    ahead_ids = ahead[24:32].astype(I32)
-    ahead_level = ahead_ids[0:1] + ahead_ids[1:2]
-    ahead_hot = one_hot(levels, ahead_level)
+    parts = [ahead[32 * d : 32 * (d + 1)] for d in range(3)]
+    groups = []
+    for directions in ((7, 5), (6,)):
+        part = jnp.concatenate([parts[d - 5] for d in directions], axis=1)
+        ids = part[24:32].astype(I32)
+        groups.append((directions, part[0:8] + part[8:16] + part[16:24], ids, one_hot(levels, ids[0:1] + ids[1:2])))
     loads[8].wait()
     for c in range(4):
         hi, lo = split2(gas_v[c].reshape(cols, levels))
         pieces[c * cols : (c + 1) * cols, :] = hi
         pieces[(4 + c) * cols : (5 + c) * cols, :] = lo
-    ahead_fluid = sampled(pieces, ahead_hot, ahead_ids[2:3], cols)
-    _, ahead_new, ahead_row = updated(ahead_now, ahead_ids[3:4] - 1, ahead_fluid, drag_t, settle_t, heat_t)
-    ahead_new = jnp.where(ahead_ids[3:4] > 0, ahead_new, 0.0)
-    for d in range(5, 8):
-        dx, dy = STEPS[d]
-        span = slice((d - 5) * capacity, (d - 4) * capacity)
-        filled, row = ahead_ids[3:4, span] > 0, ahead_row[:, span]
-        shift = jnp.where(row == 0, float(dx * si), jnp.where(row == 1, float(dy * sj), 0.0))
-        sending[d] = jnp.where(filled, ahead_new[:, span] - shift, 0.0)
-        if remote:
-            send(grain_copy(d), STEPS[d], True)
+    for directions, ahead_now, ids, ahead_hot in groups:
+        ahead_fluid = sampled(pieces, ahead_hot, ids[2:3], cols)
+        _, ahead_new, row = updated(ahead_now, ids[3:4] - 1, ahead_fluid, drag_t, settle_t, heat_t)
+        for n, d in enumerate(directions):
+            dx, dy = STEPS[d]
+            span = slice(n * capacity, (n + 1) * capacity)
+            shift = jnp.where(row == 0, float(dx * si), jnp.where(row == 1, float(dy * sj), 0.0))
+            sending[d] = jnp.where(ids[3:4] > 0, ahead_new - shift, 0.0)[:, span]
+            if remote:
+                send(grain_copy(d), STEPS[d], True)
+    if remote:
+        send(halo_copy(4), halo_steps[4], True)
 
     if remote:
         @pl.when(last)
@@ -283,14 +289,16 @@
                     out_v[c, i, j : j + 1, :] = (
                         out_v[c, i, j : j + 1, :] + mix_v[i, j : j + 1, :] * halo_y[n - 2, c, i : i + 1, :]
                     )
-    for n in (1, 0):
+    def take_gx(n, among):
         @pl.when(inside(back(halo_steps[n])))
         def _():
             halo_copy(n).wait_recv()
-            i = (0, si - 1)[n]
-            for c in range(comps):
-                out_v[c, i] = out_v[c, i] + mix_v[i] * halo_x[n, c]
-    for d in range(8):
+            side = 1 if n == 1 else 0
+            i = (0, si - 1)[side]
+            for c in among:
+                out_v[c, i] = out_v[c, i] + mix_v[i] * halo_x[side, c]
+
+    def take_grains(d):
         came = inside(back(STEPS[d]))
 
         @pl.when(came)
@@ -300,7 +308,11 @@
         @pl.when(jnp.logical_not(came))
         def _():
             landing[d] = jnp.zeros(landing.shape[1:], F32)
-    for n in range(4):
+
+    take_gx(1, range(comps))
+    for d in range(5):
+        take_grains(d)
+    for n in range(5):
         @pl.when(inside(halo_steps[n]))
         def _():
             halo_copy(n).wait_send()
@@ -308,6 +320,10 @@
         @pl.when(inside(STEPS[d]))
         def _():
             grain_copy(d).wait_send()
+    take_gx(0, range(FIRST))
+    take_gx(4, range(FIRST, comps))
+    for d in range(5, 8):
+        take_grains(d)
 
 
 def write_out(a, b, c, out_a, out_b, out_c, sems):
@@ -358,8 +374,8 @@
             pltpu.VMEM((2, comps, si, levels), F32),
             pltpu.VMEM((8, attrs, capacity), F32),
             pltpu.SemaphoreType.DMA((11,)),
-            pltpu.SemaphoreType.DMA((12,)),
-            pltpu.SemaphoreType.DMA((12,)),
+            pltpu.SemaphoreType.DMA((13,)),
+            pltpu.SemaphoreType.DMA((13,)),
             pltpu.SemaphoreType.REGULAR((3,)),
             pltpu.SemaphoreType.REGULAR,
         ],

time: 21.5 us -> 19.8 us (0.921)
  Pallas kernels: 20.7 us -> 19 us
    pallas_call x1, Pallas kernels: 19.6 us -> 17.9 us  [on_device(): pl.pallas_call(functools.partial(kernel, tiles), out_shape=(pltpu.VMEM(ga...]
where the time goes in v3:
time: 19.8 us; the launch traced here: 19.7 us
  Pallas kernels  19 us (96%)
  between operations  0.64 us (3%)
    pallas_call x1, Pallas kernels, on_device(): pl.pallas_call(functools.partial(kernel, tiles), out_shape=(pltpu.VMEM(ga...  17.9 us
    pallas_call x1, Pallas kernels, on_device(): pl.pallas_call(write_out, out_shape=shapes, in_specs=[vmem] * 3, out_spec...  1.1 us

profile of v3, /device:TPU:56, one launch (start us, length us, event | category | flops | bytes accessed | tf_op | source)
XLA Modules:
  0.0 19.7 jit_solution(5332356737970493293)
XLA Ops:
  0.6 17.9 %ash_step.1 = (f32[5,8,8,1024]{3,2,1,0:T(8,128)S(1)}, f32[8,2048]{1,0:T(8,128)S(1)}, f32[8,8,128]{2,1,0:T(8,128)S(1)}) custom-call(f32[5,8,8,1024]{3,2,1,0:T(8,128)} %gas.1, f32[8,8,1024]{2,1,0:T(8,128)} %mixing.1, f32[8,2048]{1,0:T(8,128)} %grains.1, s32[1,2048]{1,0:T(1,128)} %bitcast.4, s32[1,2048]{1,0:T(1,128)} %bitcast.5, s32[1,2048]{1,0:T(1,128)} %bitcast.6, ...), custom_call_target="tpu_custom_call" | custom-call | tf_op jit(solution)/shard_map/ash_step/pallas_call | solution.py:348
  18.6 1.1 %write_out.1 = (f32[5,8,8,1024]{3,2,1,0:T(8,128)}, f32[8,2048]{1,0:T(8,128)}, f32[8,8,128]{2,1,0:T(8,128)}) custom-call(f32[5,8,8,1024]{3,2,1,0:T(8,128)S(1)} %get-tuple-element.6.a, f32[8,2048]{1,0:T(8,128)S(1)} %get-tuple-element.7.b, f32[8,8,128]{2,1,0:T(8,128)S(1)} %get-tuple-element.8.c), custom_call_target="tpu_custom_call" | custom-call | tf_op jit(solution)/shard_map/write_out/pallas_call | solution.py:391

commit v4 on v3

--- a/solution.py
+++ b/solution.py
@@ -13,7 +13,7 @@
 BLOCK = 256
 CHUNK = 256
 RUN = 16
-FIRST = 3
+AHEAD = {0: (0, 2), 4: (2, 3), 5: (3, 5)}
 NT = (((1,), (1,)), ((), ()))
 
 
@@ -74,6 +74,19 @@
     nx, ny = tiles
     remote = nx > 1
 
+    loads = [
+        pltpu.make_async_copy(src, dst, load_sem.at[n])
+        for n, (src, dst) in enumerate(
+            (
+                (cell, cell_v), (dest, dest_v), (slot, slot_v), (kind, kind_v), (grains, grain_v),
+                (gas.at[0:4], gas_v.at[0:4]), (drag_h, drag_t), (settle_h, settle_t), (heat_h, heat_t),
+                (gas.at[4:5], gas_v.at[4:5]), (mixing, mix_v),
+            )
+        )
+    ]
+    for load in loads[:6]:
+        load.start()
+
     if remote:
         ix, iy = lax.axis_index("gx"), lax.axis_index("gy")
         place = lax.rem(ix, RUN)
@@ -113,15 +126,14 @@
         return pltpu.make_async_remote_copy(src, dst, send_sem.at[n], recv_sem.at[n], at(step), MESH)
 
     def halo_copy(n):
-        if n == 0:
-            return copy_of(0, gas.at[:FIRST, si - 1], halo_x.at[0, :FIRST], (1, 0))
-        if n == 4:
-            return copy_of(12, gas.at[FIRST:, si - 1], halo_x.at[0, FIRST:], (1, 0))
+        if n in (0, 4, 5):
+            part = slice(*AHEAD[n])
+            return copy_of(n if n == 0 else 8 + n, gas.at[part, si - 1], halo_x.at[0, part], (1, 0))
         if n == 1:
             return copy_of(1, gas.at[:, 0], halo_x.at[1], (-1, 0))
         return copy_of(n, edge_y.at[n - 2], halo_y.at[n - 2], ((0, 1), (0, -1))[n - 2])
 
-    halo_steps = ((1, 0), (-1, 0), (0, 1), (0, -1), (1, 0))
+    halo_steps = ((1, 0), (-1, 0), (0, 1), (0, -1), (1, 0), (1, 0))
 
     def grain_copy(d):
         return copy_of(4 + d, sending.at[d], landing.at[d], STEPS[d])
@@ -131,29 +143,27 @@
         def _():
             copy.start()
 
-    loads = [
-        pltpu.make_async_copy(src, dst, load_sem.at[n])
-        for n, (src, dst) in enumerate(
-            (
-                (grains, grain_v), (cell, cell_v), (kind, kind_v), (dest, dest_v), (slot, slot_v),
-                (drag_h, drag_t), (settle_h, settle_t), (heat_h, heat_t),
-                (gas.at[0:4], gas_v.at[0:4]), (gas.at[4:5], gas_v.at[4:5]), (mixing, mix_v),
-            )
-        )
-    ]
-    for load in loads:
+    if remote:
+        @pl.when(last)
+        def _():
+            pl.semaphore_wait(barrier, high)
+            halo_copy(0).start()
+    for load in loads[6:]:
         load.start()
 
     if remote:
         wide = 1 + number(place > 0) + number(place < RUN - 1)
-        pl.semaphore_wait(barrier, jnp.where(last, high, wide * high - 1))
-        send(halo_copy(0), halo_steps[0], True)
+
+        @pl.when(usual)
+        def _():
+            pl.semaphore_wait(barrier, wide * high - 1)
+        send(halo_copy(0), halo_steps[0], usual)
         greet(STEPS[5:], lambda step: last, lambda n: reply_sem.at[n])
         greet(STEPS[:3], lambda step: last, lambda n: barrier)
         greet(STEPS[5:], lambda step: (place == RUN - 2) & follows, lambda n: answer_sem)
         send(halo_copy(1), halo_steps[1], late & usual)
 
-    for load in loads[:8]:
+    for load in loads[:5]:
         load.wait()
     now, kinds, dests, cells = grain_v[...], kind_v[...], dest_v[...], cell_v[...]
     level, column = cells & (levels - 1), cells // levels
@@ -168,11 +178,12 @@
     ahead = lax.dot_general(left, slot_hot, NT, preferred_element_type=F32)
     parts = [ahead[32 * d : 32 * (d + 1)] for d in range(3)]
     groups = []
-    for directions in ((7, 5), (6,)):
+    for directions in ((7,), (5, 6)):
         part = jnp.concatenate([parts[d - 5] for d in directions], axis=1)
         ids = part[24:32].astype(I32)
         groups.append((directions, part[0:8] + part[8:16] + part[16:24], ids, one_hot(levels, ids[0:1] + ids[1:2])))
-    loads[8].wait()
+    for load in loads[5:9]:
+        load.wait()
     for c in range(4):
         hi, lo = split2(gas_v[c].reshape(cols, levels))
         pieces[c * cols : (c + 1) * cols, :] = hi
@@ -187,8 +198,9 @@
             sending[d] = jnp.where(ids[3:4] > 0, ahead_new - shift, 0.0)[:, span]
             if remote:
                 send(grain_copy(d), STEPS[d], True)
-    if remote:
-        send(halo_copy(4), halo_steps[4], True)
+                if d > 5:
+                    n = 4 if d == 7 else 5
+                    send(halo_copy(n), halo_steps[n], True)
 
     if remote:
         @pl.when(last)
@@ -312,7 +324,7 @@
     take_gx(1, range(comps))
     for d in range(5):
         take_grains(d)
-    for n in range(5):
+    for n in range(6):
         @pl.when(inside(halo_steps[n]))
         def _():
             halo_copy(n).wait_send()
@@ -320,8 +332,8 @@
         @pl.when(inside(STEPS[d]))
         def _():
             grain_copy(d).wait_send()
-    take_gx(0, range(FIRST))
-    take_gx(4, range(FIRST, comps))
+    for n in AHEAD:
+        take_gx(n, range(*AHEAD[n]))
     for d in range(5, 8):
         take_grains(d)
 
@@ -374,8 +386,8 @@
             pltpu.VMEM((2, comps, si, levels), F32),
             pltpu.VMEM((8, attrs, capacity), F32),
             pltpu.SemaphoreType.DMA((11,)),
-            pltpu.SemaphoreType.DMA((13,)),
-            pltpu.SemaphoreType.DMA((13,)),
+            pltpu.SemaphoreType.DMA((14,)),
+            pltpu.SemaphoreType.DMA((14,)),
             pltpu.SemaphoreType.REGULAR((3,)),
             pltpu.SemaphoreType.REGULAR,
         ],

time: 19.8 us -> 19.5 us (0.985)
  Pallas kernels: 19 us -> 18.7 us
    pallas_call x1, Pallas kernels: 17.9 us -> 17.6 us  [on_device(): pl.pallas_call(functools.partial(kernel, tiles), out_shape=(pltpu.VMEM(ga...]
where the time goes in v4:
time: 19.5 us; the launch traced here: 19.4 us
  Pallas kernels  18.7 us (96%)
  between operations  0.64 us (3%)
    pallas_call x1, Pallas kernels, on_device(): pl.pallas_call(functools.partial(kernel, tiles), out_shape=(pltpu.VMEM(ga...  17.6 us
    pallas_call x1, Pallas kernels, on_device(): pl.pallas_call(write_out, out_shape=shapes, in_specs=[vmem] * 3, out_spec...  1.1 us

profile of v4, /device:TPU:56, one launch (start us, length us, event | category | flops | bytes accessed | tf_op | source)
XLA Modules:
  0.0 19.4 jit_solution(12233571807303886612)
XLA Ops:
  0.6 17.6 %ash_step.1 = (f32[5,8,8,1024]{3,2,1,0:T(8,128)S(1)}, f32[8,2048]{1,0:T(8,128)S(1)}, f32[8,8,128]{2,1,0:T(8,128)S(1)}) custom-call(f32[5,8,8,1024]{3,2,1,0:T(8,128)} %gas.1, f32[8,8,1024]{2,1,0:T(8,128)} %mixing.1, f32[8,2048]{1,0:T(8,128)} %grains.1, s32[1,2048]{1,0:T(1,128)} %bitcast.4, s32[1,2048]{1,0:T(1,128)} %bitcast.5, s32[1,2048]{1,0:T(1,128)} %bitcast.6, ...), custom_call_target="tpu_custom_call" | custom-call | tf_op jit(solution)/shard_map/ash_step/pallas_call | solution.py:360
  18.3 1.1 %write_out.1 = (f32[5,8,8,1024]{3,2,1,0:T(8,128)}, f32[8,2048]{1,0:T(8,128)}, f32[8,8,128]{2,1,0:T(8,128)}) custom-call(f32[5,8,8,1024]{3,2,1,0:T(8,128)S(1)} %get-tuple-element.6.a, f32[8,2048]{1,0:T(8,128)S(1)} %get-tuple-element.7.b, f32[8,8,128]{2,1,0:T(8,128)S(1)} %get-tuple-element.8.c), custom_call_target="tpu_custom_call" | custom-call | tf_op jit(solution)/shard_map/write_out/pallas_call | solution.py:403

commit v5 on v4

--- a/solution.py
+++ b/solution.py
@@ -84,7 +84,7 @@
             )
         )
     ]
-    for load in loads[:6]:
+    for load in (loads[5], *loads[:5]):
         load.start()
 
     if remote:

time: 19.5 us -> 19.8 us (1.015)
  Pallas kernels: 18.7 us -> 19 us
    pallas_call x1, Pallas kernels: 17.6 us -> 17.9 us  [on_device(): pl.pallas_call(functools.partial(kernel, tiles), out_shape=(pltpu.VMEM(ga...]
where the time goes in v5:
time: 19.8 us; the launch traced here: 19.7 us
  Pallas kernels  19 us (96%)
  between operations  0.64 us (3%)
    pallas_call x1, Pallas kernels, on_device(): pl.pallas_call(functools.partial(kernel, tiles), out_shape=(pltpu.VMEM(ga...  17.9 us
    pallas_call x1, Pallas kernels, on_device(): pl.pallas_call(write_out, out_shape=shapes, in_specs=[vmem] * 3, out_spec...  1.1 us

profile of v5, /device:TPU:56, one launch (start us, length us, event | category | flops | bytes accessed | tf_op | source)
XLA Modules:
  0.0 19.7 jit_solution(12015198296313385717)
XLA Ops:
  0.6 17.9 %ash_step.1 = (f32[5,8,8,1024]{3,2,1,0:T(8,128)S(1)}, f32[8,2048]{1,0:T(8,128)S(1)}, f32[8,8,128]{2,1,0:T(8,128)S(1)}) custom-call(f32[5,8,8,1024]{3,2,1,0:T(8,128)} %gas.1, f32[8,8,1024]{2,1,0:T(8,128)} %mixing.1, f32[8,2048]{1,0:T(8,128)} %grains.1, s32[1,2048]{1,0:T(1,128)} %bitcast.4, s32[1,2048]{1,0:T(1,128)} %bitcast.5, s32[1,2048]{1,0:T(1,128)} %bitcast.6, ...), custom_call_target="tpu_custom_call" | custom-call | tf_op jit(solution)/shard_map/ash_step/pallas_call | solution.py:360
  18.6 1.1 %write_out.1 = (f32[5,8,8,1024]{3,2,1,0:T(8,128)}, f32[8,2048]{1,0:T(8,128)}, f32[8,8,128]{2,1,0:T(8,128)}) custom-call(f32[5,8,8,1024]{3,2,1,0:T(8,128)S(1)} %get-tuple-element.6.a, f32[8,2048]{1,0:T(8,128)S(1)} %get-tuple-element.7.b, f32[8,8,128]{2,1,0:T(8,128)S(1)} %get-tuple-element.8.c), custom_call_target="tpu_custom_call" | custom-call | tf_op jit(solution)/shard_map/write_out/pallas_call | solution.py:403
